TPU v7x, 32 devices: a whole 2x2x4 slice. The times are simulated.
32 devices in a mesh: inp: 2 (over y), pa: 4 (over x, core), pb: 4 (over z).
Axes of the slice: x: 2, y: 2, z: 4, core: 2. Of those that a mesh axis runs over, the one named last changes fastest.
Arguments:
- log_inputs: float32 [2, 256, 256, 256], P('inp', 'pa', 'pb'), may hold values from -6 to 6
- warm_potential: float32 [2, 256, 256, 256], P('inp', 'pa', 'pb'), may hold values from -6 to 6
- bary_weights: float32 [2], P('inp'), may hold values from 0.1 to 0.5
- band_reach: int32 [3], replicated, may hold values from 0 to 2, each once
- bary_cotangent: float32 [256, 256, 256], P('pa', 'pb', 'inp'), may hold values from -6 to 6
Outputs:
- barycenter: float32 [256, 256, 256], P('pa', 'pb', 'inp')
- input_grad: float32 [2, 256, 256, 256], P('inp', 'pa', 'pb')
Inputs may be any that keep to these rules, and one draw needn't show every extreme that they name: `band_reach`: a permutation of 0, 1 and 2, one entry a line direction.
All inputs are finite; a program needn't handle non-finite values.
Results may differ from a plain program's by a relative error of at most 0.00022.
Values sent between devices are 32-bit elements; how exact they have to be, the bound alone decides.
No kernel may reach another device: no remote copies, remote signals or barrier semaphores. Data moves between devices by JAX's collectives and lax.ppermute only.
A program may use at most 128 MiB of HBM per device.

v0:
```python
import math

import jax
import jax.numpy as jnp
from jax import lax
from jax.sharding import PartitionSpec as P

FORMS = ("ij,kjbc->kibc", "ij,kajc->kaic", "ij,kabj->kabi")


def line_kernel(length, reach):
    index = jnp.arange(length, dtype=jnp.int32)
    block = 4
    sigma = 3.0
    offset = (index[:, None] - index[None, :]).astype(jnp.float32)
    inside = jnp.abs(index[:, None] // block - index[None, :] // block) <= reach
    gauss = jnp.exp(-offset * offset / (2.0 * sigma * sigma)) / (sigma * math.sqrt(2.0 * math.pi))
    return 0.5 * jnp.eye(length, dtype=jnp.float32) + 0.5 * jnp.where(
        inside, gauss, jnp.zeros_like(gauss)
    )


def along_line(kernel, field, line):
    return jnp.einsum(
        FORMS[line],
        kernel,
        field,
        precision=lax.Precision.HIGHEST,
        preferred_element_type=jnp.float32,
    )


def move_once(field, source, target):
    if source == 0:
        return lax.all_to_all(field, "pa", split_axis=1, concat_axis=2, tiled=True)
    if source == 2:
        return lax.all_to_all(field, "pb", split_axis=3, concat_axis=2, tiled=True)
    if target == 2:
        return lax.all_to_all(field, "pb", split_axis=2, concat_axis=3, tiled=True)
    return lax.all_to_all(field, "pa", split_axis=2, concat_axis=1, tiled=True)


def relayout(field, source, target):
    for turn in range(abs(target - source)):
        following = source + (1 if target > source else -1)
        field = move_once(field, source, following)
        source = following
    return field


def log_conv(field, kernels, order, start, home):
    stored = []
    layout = start
    value = field
    for line in order:
        value = relayout(value, layout, line)
        layout = line
        result = jnp.log(along_line(kernels[line], jnp.exp(value), line))
        stored.append((value, result, line))
        value = result
    return (relayout(value, layout, home), stored)


def conv_adjoint(cotangent, stored, kernels, layout):
    for value, result, line in reversed(stored):
        cotangent = relayout(cotangent, layout, line)
        layout = line
        cotangent = jnp.exp(value) * along_line(kernels[line], cotangent * jnp.exp(-result), line)
    return (cotangent, layout)


def per_device(log_inputs, warm_potential, bary_weights, band_reach, bary_cotangent):
    length = log_inputs.shape[3]
    kernels = [line_kernel(length, band_reach[line]) for line in range(3)]
    weights = bary_weights[:, None, None, None]
    first_order = (2, 1, 0)
    first_home = 0
    second_order = (0, 1, 2)
    inputs_there = relayout(log_inputs, 2, first_home)
    image_one, unused_one = log_conv(warm_potential, kernels, first_order, 2, first_home)
    dual_one = inputs_there - image_one
    image_two, stored_two = log_conv(dual_one, kernels, second_order, first_home, 2)
    part_one = warm_potential + image_two
    barycenter = lax.psum_scatter(
        jnp.sum(weights * part_one, axis=0), "inp", scatter_dimension=2, tiled=True
    )
    cotangent = lax.all_gather(bary_cotangent, "inp", axis=2, tiled=True)
    one_bar = weights * cotangent[None]
    dual_one_bar, one_layout = conv_adjoint(one_bar, stored_two, kernels, 2)
    input_grad = relayout(dual_one_bar, one_layout, 2)
    return (barycenter, input_grad)


def solution(mesh):
    return jax.shard_map(
        per_device,
        mesh=mesh,
        in_specs=(
            P("inp", "pa", "pb", None),
            P("inp", "pa", "pb", None),
            P("inp"),
            P(),
            P("pa", "pb", "inp"),
        ),
        out_specs=(P("pa", "pb", "inp"), P("inp", "pa", "pb", None)),
        check_vma=False,
    )
```

profile of v0, /device:TPU:1, one launch (start us, length us, event | category | flops | bytes accessed | tf_op | source)
XLA Modules:
  0.0 1328.2 jit_solution(893937839362186486)
XLA Ops:
  7.2 9.2 copy.35
  57.3 66.1 %all-to-all-done = f32[4,1,262144]{2,1,0:T(1,128)} async-done(((f32[4,1,262144]{2,1,0:T(1,128)}), f32[4,1,262144]{2,1,0:T(1,128)}, u32[]{:S(2)}, u32[]{:S(2)}) %all-to-all-start) | async-done | bytes 4194336 | tf_op jit(solution)/shard_map/all_to_all | solution.py:37
  128.7 15.4 %reduce = f32[4,262144]{1,0:T(4,128)} reduce(f32[4,1,262144]{2,1,0:T(1,128)} %all-to-all-done, f32[]{:T(128)} %broadcast.237), dimensions={1}, to_apply=%all_to_all.106.reduce_sub_computation | reduce | bytes 8388612 | tf_op jit(solution)/shard_map/all_to_all | solution.py:37
  144.1 9.2 reshape.163
  153.4 12.0 copy.71
  165.4 10.0 copy.57
  184.0 36.9 %all-to-all-done.2 = f32[4,1,262144]{2,1,0:T(1,128)} async-done(((f32[4,1,262144]{2,1,0:T(1,128)}), f32[4,1,262144]{2,1,0:T(1,128)}, u32[]{:S(2)}, u32[]{:S(2)}) %all-to-all-start.2) | async-done | bytes 4194336 | tf_op jit(solution)/shard_map/all_to_all | solution.py:37
  227.4 15.2 %reduce.2 = f32[4,262144]{1,0:T(4,128)} reduce(f32[4,1,262144]{2,1,0:T(1,128)} %all-to-all-done.2, f32[]{:T(128)} %broadcast.237), dimensions={1}, to_apply=%all_to_all.114.reduce_sub_computation | reduce | bytes 8388612 | tf_op jit(solution)/shard_map/all_to_all | solution.py:37
  242.6 9.2 reshape.167
  260.4 12.0 copy.70
  289.6 9.1 copy.42
  312.4 15.3 %reduce.1 = f32[4,262144]{1,0:T(4,128)} reduce(f32[4,1,262144]{2,1,0:T(1,128)} %all-to-all-done.1, f32[]{:T(128)} %broadcast.237), dimensions={1}, to_apply=%all_to_all.110.reduce_sub_computation | reduce | bytes 8388612 | tf_op jit(solution)/shard_map/all_to_all | solution.py:40
  327.7 9.2 reshape.165
  336.9 9.9 copy.58
  346.8 11.7 copy.39
  367.0 15.4 %reduce.3 = f32[4,262144]{1,0:T(4,128)} reduce(f32[4,1,262144]{2,1,0:T(1,128)} %all-to-all-done.3, f32[]{:T(128)} %broadcast.237), dimensions={1}, to_apply=%all_to_all.115.reduce_sub_computation | reduce | bytes 8388612 | tf_op jit(solution)/shard_map/all_to_all | solution.py:40
  382.4 9.2 reshape.169
  400.3 9.9 copy.43
  434.9 9.1 copy.44
  452.7 52.8 %all_to_all.144 = f32[4,1,262144]{2,1,0:T(1,128)} all-to-all(f32[4,1,262144]{2,1,0:T(1,128)} %reshape.170), channel_id=1, replica_groups=mesh['inp'=2,'pa'=4,'pb'=4] {'pa'}, dimensions={0} | all-to-all | bytes 8388608 | tf_op jit(solution)/shard_map/all_to_all | solution.py:35
  505.5 15.2 %reduce.4 = f32[4,262144]{1,0:T(4,128)} reduce(f32[4,1,262144]{2,1,0:T(1,128)} %all_to_all.144, f32[]{:T(128)} %broadcast.237), dimensions={1}, to_apply=%all_to_all.116.reduce_sub_computation | reduce | bytes 8388612 | tf_op jit(solution)/shard_map/all_to_all | solution.py:35
  520.7 9.2 reshape.171
  538.5 9.9 copy.45
  589.5 91.3 %all-to-all-done.5 = f32[4,1,262144]{2,1,0:T(1,128)} async-done(((f32[4,1,262144]{2,1,0:T(1,128)}), f32[4,1,262144]{2,1,0:T(1,128)}, u32[]{:S(2)}, u32[]{:S(2)}) %all-to-all-start.5) | async-done | bytes 4194336 | tf_op jit(solution)/shard_map/all_to_all | solution.py:39
  680.8 15.4 %reduce.5 = f32[4,262144]{1,0:T(4,128)} reduce(f32[4,1,262144]{2,1,0:T(1,128)} %all-to-all-done.5, f32[]{:T(128)} %broadcast.237), dimensions={1}, to_apply=%all_to_all.117.reduce_sub_computation | reduce | bytes 8388612 | tf_op jit(solution)/shard_map/all_to_all | solution.py:39
  696.2 9.3 reshape.173
  714.1 12.0 copy.69
  743.4 11.4 multiply_bitcast_fusion
  786.1 84.1 %all-to-all-done.6 = f32[4,1,262144]{2,1,0:T(1,128)} async-done(((f32[4,1,262144]{2,1,0:T(1,128)}), f32[4,1,262144]{2,1,0:T(1,128)}, u32[]{:S(2)}, u32[]{:S(2)}) %all-to-all-start.6) | async-done | bytes 4194336 | tf_op jit(solution)/shard_map/all_to_all | solution.py:37
  870.3 15.4 %reduce.6 = f32[4,262144]{1,0:T(4,128)} reduce(f32[4,1,262144]{2,1,0:T(1,128)} %all-to-all-done.6, f32[]{:T(128)} %broadcast.237), dimensions={1}, to_apply=%all_to_all.118.reduce_sub_computation | reduce | bytes 8388612 | tf_op jit(solution)/shard_map/all_to_all | solution.py:37
  885.6 9.3 reshape.175
  894.9 12.0 copy.68
  915.6 11.0 bitcast_multiply_fusion.1
  926.6 9.1 copy.50
  944.4 54.5 %all_to_all.145 = f32[4,1,262144]{2,1,0:T(1,128)} all-to-all(f32[4,1,262144]{2,1,0:T(1,128)} %reshape.176), channel_id=1, replica_groups=mesh['inp'=2,'pa'=4,'pb'=4] {'pa'}, dimensions={0} | all-to-all | bytes 8388608 | tf_op jit(solution)/shard_map/all_to_all | solution.py:40
  998.9 15.2 %reduce.7 = f32[4,262144]{1,0:T(4,128)} reduce(f32[4,1,262144]{2,1,0:T(1,128)} %all_to_all.145, f32[]{:T(128)} %broadcast.237), dimensions={1}, to_apply=%all_to_all.122.reduce_sub_computation | reduce | bytes 8388612 | tf_op jit(solution)/shard_map/all_to_all | solution.py:40
  1014.1 9.3 reshape.177
  1023.4 9.9 copy.51
  1042.3 11.1 bitcast_multiply_fusion
  1083.7 40.7 %all-to-all-done.8 = f32[4,1,262144]{2,1,0:T(1,128)} async-done(((f32[4,1,262144]{2,1,0:T(1,128)}), f32[4,1,262144]{2,1,0:T(1,128)}, u32[]{:S(2)}, u32[]{:S(2)}) %all-to-all-start.8) | async-done | bytes 4194336 | tf_op jit(solution)/shard_map/all_to_all | solution.py:35
  1124.4 15.4 %reduce.8 = f32[4,262144]{1,0:T(4,128)} reduce(f32[4,1,262144]{2,1,0:T(1,128)} %all-to-all-done.8, f32[]{:T(128)} %broadcast.237), dimensions={1}, to_apply=%all_to_all.126.reduce_sub_computation | reduce | bytes 8388612 | tf_op jit(solution)/shard_map/all_to_all | solution.py:35
  1139.8 9.2 reshape.179
  1149.1 9.9 copy.53
  1159.0 10.0 copy.59
  1177.6 98.3 %all_to_all.146 = f32[4,1,262144]{2,1,0:T(1,128)} all-to-all(f32[4,1,262144]{2,1,0:T(1,128)} %reshape.180), channel_id=1, replica_groups=mesh['inp'=2,'pa'=4,'pb'=4] {'pb'}, dimensions={0} | all-to-all | bytes 8388608 | tf_op jit(solution)/shard_map/all_to_all | solution.py:39
  1275.9 15.5 %reduce.9 = f32[4,262144]{1,0:T(4,128)} reduce(f32[4,1,262144]{2,1,0:T(1,128)} %all_to_all.146, f32[]{:T(128)} %broadcast.237), dimensions={1}, to_apply=%all_to_all.130.reduce_sub_computation | reduce | bytes 8388612 | tf_op jit(solution)/shard_map/all_to_all | solution.py:39
  1291.4 9.3 reshape.181
  1300.6 12.0 copy.67
  (56 shorter events, 331.4 us)
Async XLA Ops:
  24.9 5.6 copy-start.1
  24.9 98.4 %all-to-all-start = ((f32[4,1,262144]{2,1,0:T(1,128)}), f32[4,1,262144]{2,1,0:T(1,128)}, u32[]{:S(2)}, u32[]{:S(2)}) async-start(f32[4,1,262144]{2,1,0:T(1,128)} %reshape.162), calls=%async_computation | async-start | bytes 8388608 | tf_op jit(solution)/shard_map/all_to_all | solution.py:37
  123.3 97.5 %all-to-all-start.2 = ((f32[4,1,262144]{2,1,0:T(1,128)}), f32[4,1,262144]{2,1,0:T(1,128)}, u32[]{:S(2)}, u32[]{:S(2)}) async-start(f32[4,1,262144]{2,1,0:T(1,128)} %reshape.166), calls=%async_computation.2 | async-start | bytes 8388608 | tf_op jit(solution)/shard_map/all_to_all | solution.py:37
  220.9 86.5 %all-to-all-start.1 = ((f32[4,1,262144]{2,1,0:T(1,128)}), f32[4,1,262144]{2,1,0:T(1,128)}, u32[]{:S(2)}, u32[]{:S(2)}) async-start(f32[4,1,262144]{2,1,0:T(1,128)} %reshape.164), calls=%async_computation.1 | async-start | bytes 8388608 | tf_op jit(solution)/shard_map/all_to_all | solution.py:40
  307.4 59.7 %all-to-all-start.3 = ((f32[4,1,262144]{2,1,0:T(1,128)}), f32[4,1,262144]{2,1,0:T(1,128)}, u32[]{:S(2)}, u32[]{:S(2)}) async-start(f32[4,1,262144]{2,1,0:T(1,128)} %reshape.168), calls=%async_computation.3 | async-start | bytes 8388608 | tf_op jit(solution)/shard_map/all_to_all | solution.py:40
  426.6 2.0 copy-start
  583.2 97.6 %all-to-all-start.5 = ((f32[4,1,262144]{2,1,0:T(1,128)}), f32[4,1,262144]{2,1,0:T(1,128)}, u32[]{:S(2)}, u32[]{:S(2)}) async-start(f32[4,1,262144]{2,1,0:T(1,128)} %reshape.172), calls=%async_computation.5 | async-start | bytes 8388608 | tf_op jit(solution)/shard_map/all_to_all | solution.py:39
  588.1 155.3 %all-gather.2.cloned.1.call-start = ((), (), s32[]{:S(2)}) async-start(), calls=%async_computation.12 | async-start | bytes 6291456 | tf_op jit(solution)/shard_map/all_gather | solution.py:87
  772.6 97.6 %all-to-all-start.6 = ((f32[4,1,262144]{2,1,0:T(1,128)}), f32[4,1,262144]{2,1,0:T(1,128)}, u32[]{:S(2)}, u32[]{:S(2)}) async-start(f32[4,1,262144]{2,1,0:T(1,128)} %reshape.174), calls=%async_computation.7 | async-start | bytes 8388608 | tf_op jit(solution)/shard_map/all_to_all | solution.py:37
  1071.1 53.3 %all-to-all-start.8 = ((f32[4,1,262144]{2,1,0:T(1,128)}), f32[4,1,262144]{2,1,0:T(1,128)}, u32[]{:S(2)}, u32[]{:S(2)}) async-start(f32[4,1,262144]{2,1,0:T(1,128)} %reshape.178), calls=%async_computation.9 | async-start | bytes 8388608 | tf_op jit(solution)/shard_map/all_to_all | solution.py:35
  1077.0 244.2 %reduce-scatter.2.cloned.1.call-start = ((), (), s32[]{:S(2)}) async-start(), calls=%async_computation.11 | async-start | bytes 6291456 | tf_op jit(solution)/shard_map/reduce_scatter | solution.py:84
Sparse Core Ops, SparseCore 0:
  590.5 57.7 all-gather.1
  1083.8 53.4 reduce-scatter.1
where the time goes:
time: 1340 us; the launch traced here: 1330 us
  local copies, waits for them, and re-layouts  509 us (38%)
  waiting for transfers between devices  320 us (24%)
  blocking collectives  206 us (15%)
  other arithmetic  160 us (12%)
  matrix products  81 us (6%)
  starting transfers between devices  37.7 us (3%)
  between operations  15 us (1%)
    unnamed x25, local copies, waits for them, and re-layouts  190 us
    all_to_all x3, waiting for transfers between devices, move_once(): return lax.all_to_all(field, 'pb', split_axis=3, concat_axis=2, tiled=True)  187 us
    exp x13, local copies, waits for them, and re-layouts, log_conv(): result = jnp.log(along_line(kernels[line], jnp.exp(value), line))  122 us
    all_to_all x1, blocking collectives, move_once(): return lax.all_to_all(field, 'pb', split_axis=2, concat_axis=3, tiled=True)  98.3 us
    all_to_all x1, waiting for transfers between devices, move_once(): return lax.all_to_all(field, 'pb', split_axis=2, concat_axis=3, tiled=True)  91.3 us
    dot_general x9, matrix products, along_line(): jnp.einsum(FORMS[line], kernel, field, precision=lax.Precision.HIGHEST, p...  81 us
    all_to_all x1, blocking collectives, move_once(): return lax.all_to_all(field, 'pa', split_axis=2, concat_axis=1, tiled=True)  54.5 us
    all_to_all x1, blocking collectives, move_once(): return lax.all_to_all(field, 'pa', split_axis=1, concat_axis=2, tiled=True)  52.8 us
  transfers between devices with their start and end apart: 9, of which 5 were waited for; matrix products, arithmetic and copies ran while one was open for 28% of the time, Pallas kernels for 0%

commit v1 on v0

v1 whole, which is shorter than its diff:
```python
import functools
import math

import jax
import jax.numpy as jnp
from jax import lax
from jax.experimental import pallas as pl
from jax.experimental.pallas import tpu as pltpu
from jax.sharding import PartitionSpec as P

BLOCK = 4
SIGMA = 3.0
HALO = 2 * BLOCK
XOUT = 16
SUB = 8
F32 = jnp.float32
BF16 = jnp.bfloat16


def weight(i, j, reach):
    offset = (i - j).astype(F32)
    inside = jnp.abs(i // BLOCK - j // BLOCK) <= reach
    gauss = jnp.exp(-offset * offset / (2.0 * SIGMA * SIGMA)) / (SIGMA * math.sqrt(2.0 * math.pi))
    return jnp.where(i == j, 0.5, 0.0) + 0.5 * jnp.where(inside, gauss, 0.0)


def halves(value):
    high = value.astype(BF16)
    return high, (value - high.astype(F32)).astype(BF16)


def dot(a, b):
    return jnp.dot(a, b, preferred_element_type=F32)


def iotas(shape):
    return (lax.broadcasted_iota(jnp.int32, shape, 0), lax.broadcasted_iota(jnp.int32, shape, 1))


def fill_z(ref, reach):
    n = ref.shape[1]
    i, j = iotas((n, n))
    high, low = halves(weight(i, j, reach))
    ref[0:n] = high
    ref[n : 2 * n] = high
    ref[2 * n : 3 * n] = low


def fill_y(ref, reach):
    n = ref.shape[0]
    m = n + 2 * HALO
    i, c = iotas((n, 3 * m))
    part = jnp.where(c >= 2 * m, 2, jnp.where(c >= m, 1, 0))
    c = c - part * m
    j = jnp.where(c < n, c + HALO, jnp.where(c < n + HALO, c - n, c))
    value = weight(i + HALO, j, reach)
    high = value.astype(BF16).astype(F32)
    ref[...] = jnp.where(part == 2, value - high, high).astype(BF16)


def fill_x(ref, reach):
    m = (XOUT + 2 * HALO) * SUB
    r, c = iotas((XOUT * SUB, m))
    value = weight(r // SUB + HALO, c // SUB, reach)
    value = jnp.where(r % SUB == c % SUB, value, 0.0)
    high, low = halves(value)
    ref[:, 0:m] = high
    ref[:, m : 2 * m] = high
    ref[:, 2 * m : 3 * m] = low


def z_product(rows, kz):
    high, low = halves(rows)
    return dot(jnp.concatenate([high, low, high], axis=1), kz[...])


class Copies:
    def __init__(self, sems):
        self.sems = sems
        self.used = 0

    def start(self, src, dst):
        copy = pltpu.make_async_copy(src, dst, self.sems.at[self.used])
        self.used += 1
        copy.start()
        return copy


def strips_out(copies, buf, outs):
    nx, ny, _ = buf.shape
    xs = (pl.ds(0, HALO), pl.ds(nx - HALO, HALO))
    ys = (pl.ds(0, HALO), pl.ds(ny - HALO, HALO))
    started = []
    for n, x in enumerate(xs):
        started.append(copies.start(buf.at[x], outs[n]))
    for n, y in enumerate(ys):
        started.append(copies.start(buf.at[:, y], outs[2 + n]))
    for n, (x, y) in enumerate(((x, y) for x in xs for y in ys)):
        started.append(copies.start(buf.at[x, y], outs[4 + n]))
    return started


def strip_shapes(nx, ny, nz):
    shapes = [(HALO, ny, nz)] * 2 + [(nx, HALO, nz)] * 2 + [(HALO, HALO, nz)] * 4
    return [jax.ShapeDtypeStruct(s, F32) for s in shapes]


def first_kernel(reach, warm, u_out, *rest):
    outs, (buf, ubuf, kz, sems) = rest[:8], rest[8:]
    nx, ny, nz = buf.shape
    step = 8
    copies = Copies(sems)
    loads = [copies.start(warm.at[pl.ds(x, step)], buf.at[pl.ds(x, step)]) for x in range(0, nx, step)]
    fill_z(kz, reach[2])
    started = []
    for n, x in enumerate(range(0, nx, step)):
        loads[n].wait()
        rows = jnp.exp(buf[x : x + step].reshape(step * ny, nz))
        ubuf[x : x + step] = z_product(rows, kz).reshape(step, ny, nz)
        started.append(copies.start(ubuf.at[pl.ds(x, step)], u_out.at[pl.ds(x, step)]))
    started += strips_out(copies, ubuf, outs)
    for copy in started:
        copy.wait()


def load_halo(copies, u, halos, buf):
    nx, ny, _ = u.shape
    own_x, own_y = pl.ds(HALO, nx), pl.ds(0, ny)
    xs = (pl.ds(0, HALO), pl.ds(HALO + nx, HALO))
    ys = (pl.ds(ny, HALO), pl.ds(ny + HALO, HALO))
    loads = [copies.start(u, buf.at[own_x, own_y])]
    for n, x in enumerate(xs):
        loads.append(copies.start(halos[n], buf.at[x, own_y]))
    for n, y in enumerate(ys):
        loads.append(copies.start(halos[2 + n], buf.at[own_x, y]))
    for n, (x, y) in enumerate(((x, y) for x in xs for y in ys)):
        loads.append(copies.start(halos[4 + n], buf.at[x, y]))
    return loads


def y_products(buf, vbuf, ky):
    unroll = 4

    def body(step, carry):
        for n in range(unroll):
            x = step * unroll + n
            high, low = halves(buf[x])
            vbuf[x] = dot(ky[...], jnp.concatenate([high, low, high], axis=0))
        return carry

    lax.fori_loop(0, buf.shape[0] // unroll, body, 0)


def x_products(vbuf, kx, tile, store):
    nz = vbuf.shape[2]
    span = XOUT + 2 * HALO
    for x in range(0, vbuf.shape[0] - 2 * HALO, XOUT):
        window = vbuf[x : x + span, pl.ds(tile * SUB, SUB), :].reshape(span * SUB, nz)
        high, low = halves(window)
        store(x, dot(kx[...], jnp.concatenate([high, low, high], axis=0)))


def second_kernel(reach, u, *rest):
    halos, (log_in, d_out, u_out), outs = rest[:8], rest[8:11], rest[11:19]
    buf, vbuf, lbuf, dbuf, ubuf, kx, ky, kz, sems = rest[19:]
    nx, ny, nz = ubuf.shape
    copies = Copies(sems)
    loads = load_halo(copies, u, halos, buf)
    late = copies.start(log_in, lbuf)
    fill_x(kx, reach[0])
    fill_y(ky, reach[1])
    fill_z(kz, reach[2])
    for copy in loads:
        copy.wait()
    y_products(buf, vbuf, ky)
    late.wait()

    def body(tile, carry):
        rows = pl.ds(pl.multiple_of(tile * SUB, SUB), SUB)

        def store(x, product):
            value = jnp.exp(lbuf[x : x + XOUT, rows, :].reshape(XOUT * SUB, nz)) / product
            dbuf[x : x + XOUT, rows, :] = value.reshape(XOUT, SUB, nz)

        x_products(vbuf, kx, tile, store)
        d = dbuf[:, rows, :].reshape(nx * SUB, nz)
        ubuf[:, rows, :] = z_product(d, kz).reshape(nx, SUB, nz)
        return carry

    lax.fori_loop(0, ny // SUB, body, 0)
    started = strips_out(copies, ubuf, outs)
    started.append(copies.start(ubuf, u_out))
    started.append(copies.start(dbuf, d_out))
    for copy in started:
        copy.wait()


def third_kernel(reach, side, weights, u, *rest):
    halos, (warm, own_cot, far_cot, keep_out, send_out, u_out), outs = rest[:8], rest[8:14], rest[14:22]
    buf, vbuf, wbuf, cbuf, fbuf, kbuf, sbuf, qbuf, ubuf, kx, ky, kz, sems = rest[22:]
    nx, ny, nz = ubuf.shape
    half = nz // 2
    copies = Copies(sems)
    loads = load_halo(copies, u, halos, buf)
    late = [copies.start(warm, wbuf), copies.start(own_cot, cbuf), copies.start(far_cot, fbuf)]
    fill_x(kx, reach[0])
    fill_y(ky, reach[1])
    fill_z(kz, reach[2])
    for copy in loads:
        copy.wait()
    y_products(buf, vbuf, ky)
    for copy in late:
        copy.wait()
    first = side[0] == 0
    scale = weights[0]

    def body(tile, carry):
        rows = pl.ds(pl.multiple_of(tile * SUB, SUB), SUB)

        def store(x, product):
            planes = slice(x, x + XOUT)
            part = scale * (wbuf[planes, rows, :].reshape(XOUT * SUB, nz) + jnp.log(product))
            left, right = part[:, :half], part[:, half:]
            kbuf[planes, rows, :] = jnp.where(first, left, right).reshape(XOUT, SUB, half)
            sbuf[planes, rows, :] = jnp.where(first, right, left).reshape(XOUT, SUB, half)
            own = cbuf[planes, rows, :].reshape(XOUT * SUB, half)
            far = fbuf[planes, rows, :].reshape(XOUT * SUB, half)
            cot = jnp.concatenate([jnp.where(first, own, far), jnp.where(first, far, own)], axis=1)
            qbuf[planes, rows, :] = (scale * cot / product).reshape(XOUT, SUB, nz)

        x_products(vbuf, kx, tile, store)
        q = qbuf[:, rows, :].reshape(nx * SUB, nz)
        ubuf[:, rows, :] = z_product(q, kz).reshape(nx, SUB, nz)
        return carry

    lax.fori_loop(0, ny // SUB, body, 0)
    started = [copies.start(sbuf, send_out)]
    started += strips_out(copies, ubuf, outs)
    started.append(copies.start(ubuf, u_out))
    started.append(copies.start(kbuf, keep_out))
    for copy in started:
        copy.wait()


def last_kernel(reach, u, *rest):
    halos, (d, g_out) = rest[:8], rest[8:10]
    buf, vbuf, dbuf, gbuf, kx, ky, sems = rest[10:]
    nx, ny, nz = gbuf.shape
    copies = Copies(sems)
    loads = load_halo(copies, u, halos, buf)
    late = copies.start(d, dbuf)
    fill_x(kx, reach[0])
    fill_y(ky, reach[1])
    for copy in loads:
        copy.wait()
    y_products(buf, vbuf, ky)
    late.wait()

    def body(tile, carry):
        rows = pl.ds(pl.multiple_of(tile * SUB, SUB), SUB)

        def store(x, product):
            planes = slice(x, x + XOUT)
            gbuf[planes, rows, :] = dbuf[planes, rows, :] * product.reshape(XOUT, SUB, nz)

        x_products(vbuf, kx, tile, store)
        return carry

    lax.fori_loop(0, ny // SUB, body, 0)
    copies.start(gbuf, g_out).wait()


def add_kernel(a, b, out):
    out[...] = a[...] + b[...]


SMEM = pl.BlockSpec(memory_space=pltpu.SMEM)
ANY = pl.BlockSpec(memory_space=pl.ANY)


def call(kernel, name, scalars, arrays, out_shape, scratch, copies, flops):
    moved = sum(math.prod(a.shape) * 4 for a in list(arrays) + list(out_shape))
    return pl.pallas_call(
        kernel,
        name=name,
        out_shape=out_shape,
        in_specs=[SMEM] * len(scalars) + [ANY] * len(arrays),
        out_specs=[ANY] * len(out_shape),
        scratch_shapes=scratch + [pltpu.SemaphoreType.DMA((copies,))],
        compiler_params=pltpu.CompilerParams(vmem_limit_bytes=52 * 2**20),
        cost_estimate=pl.CostEstimate(flops=flops, bytes_accessed=moved, transcendentals=0),
    )(*scalars, *arrays)


def shift(value, sizes, dx, dy):
    na, nb = sizes
    perm = []
    for a in range(na):
        for b in range(nb):
            if 0 <= a + dx < na and 0 <= b + dy < nb:
                perm.append((a * nb + b, (a + dx) * nb + b + dy))
    return lax.ppermute(value, ("pa", "pb"), perm)


def exchange(strips, sizes):
    x0, x1, y0, y1, c00, c01, c10, c11 = strips
    return [
        shift(x1, sizes, 1, 0),
        shift(x0, sizes, -1, 0),
        shift(y1, sizes, 0, 1),
        shift(y0, sizes, 0, -1),
        shift(c11, sizes, 1, 1),
        shift(c10, sizes, 1, -1),
        shift(c01, sizes, -1, 1),
        shift(c00, sizes, -1, -1),
    ]


def per_device(sizes, log_inputs, warm_potential, bary_weights, band_reach, bary_cotangent):
    _, nx, ny, nz = log_inputs.shape
    half = nz // 2
    log_inputs = log_inputs.reshape(nx, ny, nz)
    warm = warm_potential.reshape(nx, ny, nz)
    side = lax.axis_index("inp").astype(jnp.int32).reshape(1)
    swap = [(0, 1), (1, 0)]

    own = (nx, ny, nz)
    wide = (nx + 2 * HALO, ny + 2 * HALO, nz)
    tall = (nx + 2 * HALO, ny, nz)
    half_shape = (nx, ny, half)
    full = jax.ShapeDtypeStruct(own, F32)
    part = jax.ShapeDtypeStruct(half_shape, F32)
    strips_like = strip_shapes(nx, ny, nz)
    vmem = lambda shape: pltpu.VMEM(shape, F32)
    span = (XOUT + 2 * HALO) * SUB
    kx = pltpu.VMEM((XOUT * SUB, 3 * span), BF16)
    ky = pltpu.VMEM((ny, 3 * (ny + 2 * HALO)), BF16)
    kz = pltpu.VMEM((3 * nz, nz), BF16)
    lines = nx * ny * nz
    z_flops = 2 * 3 * lines * nz
    xy_flops = 2 * 3 * lines * (ny + span)

    far_cot = lax.ppermute(bary_cotangent, "inp", swap)
    u, *strips = call(
        first_kernel, "z_lines", (band_reach,), (warm,), [full] + strips_like,
        [vmem(own), vmem(own), kz], 2 * (nx // 8) + 8, z_flops,
    )
    halos = exchange(strips, sizes)
    d, u, *strips = call(
        second_kernel, "dual", (band_reach,), (u, *halos, log_inputs), [full, full] + strips_like,
        [vmem(wide), vmem(tall), vmem(own), vmem(own), vmem(own), kx, ky, kz], 20, z_flops + xy_flops,
    )
    halos = exchange(strips, sizes)
    keep, send, u, *strips = call(
        third_kernel, "partial", (band_reach, side, bary_weights), (u, *halos, warm, bary_cotangent, far_cot),
        [part, part, full] + strips_like,
        [vmem(wide), vmem(tall), vmem(own)] + [vmem(half_shape)] * 4 + [vmem(own), vmem(own), kx, ky, kz],
        23, z_flops + xy_flops,
    )
    arrived = lax.ppermute(send, "inp", swap)
    halos = exchange(strips, sizes)
    (grad,) = call(
        last_kernel, "gradient", (band_reach,), (u, *halos, d), [full],
        [vmem(wide), vmem(tall), vmem(own), vmem(own), kx, ky], 11, xy_flops,
    )
    step = 8
    block = pl.BlockSpec((step, ny, half), lambda n: (n, 0, 0))
    barycenter = pl.pallas_call(
        add_kernel, name="barycenter", out_shape=part, grid=(nx // step,),
        in_specs=[block, block], out_specs=block,
        cost_estimate=pl.CostEstimate(flops=lines // 2, bytes_accessed=6 * lines, transcendentals=0),
    )(keep, arrived)
    return (barycenter, grad.reshape(1, nx, ny, nz))


def solution(mesh):
    sizes = (mesh.shape["pa"], mesh.shape["pb"])
    return jax.shard_map(
        functools.partial(per_device, sizes),
        mesh=mesh,
        in_specs=(
            P("inp", "pa", "pb", None),
            P("inp", "pa", "pb", None),
            P("inp"),
            P(),
            P("pa", "pb", "inp"),
        ),
        out_specs=(P("pa", "pb", "inp"), P("inp", "pa", "pb", None)),
        check_vma=False,
    )
```

time: 1340 us -> 176 us (0.13)
  local copies, waits for them, and re-layouts: 509 us -> 4.91 us
  waiting for transfers between devices: 320 us -> 40 us
  blocking collectives: 206 us -> 0 us
  other arithmetic: 160 us -> 0 us
  matrix products: 81 us -> 0 us
  Pallas kernels: 0 us -> 58.8 us
  starting transfers between devices: 37.7 us -> 68.8 us
    all_to_all x7 -> x0, waiting for transfers between devices: 319 us -> none  [the longest x3 187 us: move_once(): return lax.all_to_all(field, 'pb', split_axis=3, concat_axis=2, tiled=True)]
    all_to_all x3 -> x0, blocking collectives: 206 us -> none  [the longest x1 98.3 us: move_once(): return lax.all_to_all(field, 'pb', split_axis=2, concat_axis=3, tiled=True)]
    unnamed x25 -> x18, local copies, waits for them, and re-layouts: 190 us -> 4.91 us
    all_to_all x10 -> x0, other arithmetic: 153 us -> none  [the longest x3 46 us: move_once(): return lax.all_to_all(field, 'pb', split_axis=3, concat_axis=2, tiled=True)]
    all_to_all x14 -> x0, local copies, waits for them, and re-layouts: 133 us -> none  [the longest x5 49 us: move_once(): return lax.all_to_all(field, 'pa', split_axis=2, concat_axis=1, tiled=True)]
    exp x13 -> x0, local copies, waits for them, and re-layouts: 122 us -> none  [log_conv(): result = jnp.log(along_line(kernels[line], jnp.exp(value), line))]
    dot_general x9 -> x0, matrix products: 81 us -> none  [along_line(): jnp.einsum(FORMS[line], kernel, field, precision=lax.Precision.HIGHEST, p...]
    ppermute x0 -> x26, starting transfers between devices: none -> 68.8 us  [the longest x24 66.4 us: shift(): return lax.ppermute(value, ('pa', 'pb'), perm)]
  transfers between devices with their start and end apart: 9 -> 26, of which waited for: 5 -> 9; matrix products, arithmetic and copies ran while one was open for 28% -> 0% of each run, Pallas kernels for 0% -> 21%
where the time goes in v1:
time: 176 us; the launch traced here: 174 us
  starting transfers between devices  68.8 us (39%)
  Pallas kernels  58.8 us (33%)
  waiting for transfers between devices  40 us (23%)
  local copies, waits for them, and re-layouts  4.91 us (3%)
    ppermute x24, starting transfers between devices, shift(): return lax.ppermute(value, ('pa', 'pb'), perm)  66.4 us
    pallas_call x4, Pallas kernels, call(): pl.pallas_call(kernel, name=name, out_shape=out_shape, in_specs=[SMEM] *...  52.7 us
    ppermute x24, waiting for transfers between devices, shift(): return lax.ppermute(value, ('pa', 'pb'), perm)  40 us
    pallas_call x1, Pallas kernels, per_device(): pl.pallas_call(add_kernel, name='barycenter', out_shape=part, grid=(nx //...  6.04 us
    unnamed x18, local copies, waits for them, and re-layouts  4.91 us
  transfers between devices with their start and end apart: 26, of which 9 were waited for; matrix products, arithmetic and copies ran while one was open for 0% of the time, Pallas kernels for 21%

profile of v1, /device:TPU:1, one launch (start us, length us, event | category | flops | bytes accessed | tf_op | source)
XLA Modules:
  0.0 174.1 jit_solution(9481724099010961407)
XLA Ops:
  0.6 2.1 %collective-permute-start.16 = (f32[64,64,128]{2,1,0:T(8,128)}, f32[64,64,128]{2,1,0:T(8,128)S(1)}, u32[]{:S(2)}, u32[]{:S(2)}) collective-permute-start(f32[64,64,128]{2,1,0:T(8,128)} %rest_9_.1), channel_id=1, source_target_pairs={{0,16},{16,0},{1,17},{17,1},{2,18},{18,2},{3,19},{19,3},{4,20},{20... | collective-permute-start | bytes 6291464 | tf_op jit(solution)/shard_map/ppermute | solution.py:343
  2.8 0.7 copy-done
  3.4 7.2 %z_lines.1 = (f32[64,64,256]{2,1,0:T(8,128)}, f32[8,64,256]{2,1,0:T(8,128)S(1)}, f32[8,64,256]{2,1,0:T(8,128)S(1)}, f32[64,8,256]{2,1,0:T(8,128)S(1)}, f32[64,8,...) custom-call(s32[3]{0:T(128)S(1)} %copy-done, ...), custom_call_target="tpu_custom_call" | custom-call | flops 1610612736 | bytes 10747904 | tf_op jit(solution)/shard_map/z_lines/pallas_call | solution.py:283
  10.6 5.0 %collective-permute-start.4 = (f32[8,8,256]{2,1,0:T(8,128)S(1)}, f32[8,8,256]{2,1,0:T(8,128)S(1)}, u32[]{:S(2)}, u32[]{:S(2)}) collective-permute-start(f32[8,8,256]{2,1,0:T(8,128)S(1)} %get-tuple-element.37), channel_id=1, source_target_pairs={{0,5},{1,6},{2,7},{4,9},{5,10},{6,11},{8,13},{9,14},{10,15},{16,21... | collective-permute-start | bytes 196616 | tf_op jit(solution)/shard_map/ppermute | solution.py:302
  15.6 1.3 collective-permute-start.5
  16.9 4.3 %collective-permute-start.6 = (f32[8,8,256]{2,1,0:T(8,128)S(1)}, f32[8,8,256]{2,1,0:T(8,128)S(1)}, u32[]{:S(2)}, u32[]{:S(2)}) collective-permute-start(f32[8,8,256]{2,1,0:T(8,128)S(1)} %get-tuple-element.39), channel_id=1, source_target_pairs={{4,1},{5,2},{6,3},{8,5},{9,6},{10,7},{12,9},{13,10},{14,11},{20,17... | collective-permute-start | bytes 196616 | tf_op jit(solution)/shard_map/ppermute | solution.py:302
  21.2 1.3 collective-permute-start.7
  22.5 0.0 collective-permute-done.4.rest_4_
  22.5 2.9 %collective-permute-start = (f32[8,64,256]{2,1,0:T(8,128)S(1)}, f32[8,64,256]{2,1,0:T(8,128)S(1)}, u32[]{:S(2)}, u32[]{:S(2)}) collective-permute-start(f32[8,64,256]{2,1,0:T(8,128)S(1)} %get-tuple-element.33), channel_id=1, source_target_pairs={{0,4},{1,5},{2,6},{3,7},{4,8},{5,9},{6,10},{7,11},{8,12},{9,13},{1... | collective-permute-start | bytes 1572872 | tf_op jit(solution)/shard_map/ppermute | solution.py:302
  25.4 0.0 collective-permute-done.5.rest_5_
  25.5 1.9 %collective-permute-start.1 = (f32[8,64,256]{2,1,0:T(8,128)S(1)}, f32[8,64,256]{2,1,0:T(8,128)S(1)}, u32[]{:S(2)}, u32[]{:S(2)}) collective-permute-start(f32[8,64,256]{2,1,0:T(8,128)S(1)} %get-tuple-element.34), channel_id=1, source_target_pairs={{4,0},{5,1},{6,2},{7,3},{8,4},{9,5},{10,6},{11,7},{12,8},{13,9},{1... | collective-permute-start | bytes 1572872 | tf_op jit(solution)/shard_map/ppermute | solution.py:302
  27.4 4.5 %collective-permute-start.2 = (f32[64,8,256]{2,1,0:T(8,128)}, f32[64,8,256]{2,1,0:T(8,128)S(1)}, u32[]{:S(2)}, u32[]{:S(2)}) collective-permute-start(f32[64,8,256]{2,1,0:T(8,128)} %get-tuple-element.35), channel_id=1, source_target_pairs={{0,1},{1,2},{2,3},{4,5},{5,6},{6,7},{8,9},{9,10},{10,11},{12,13},{... | collective-permute-start | bytes 1572872 | tf_op jit(solution)/shard_map/ppermute | solution.py:302
  31.9 0.0 collective-permute-done.7.rest_7_
  31.9 1.3 collective-permute-start.3
  33.2 3.1 %collective-permute-done.1.rest_1_ = f32[8,64,256]{2,1,0:T(8,128)S(1)} collective-permute-done((f32[8,64,256]{2,1,0:T(8,128)S(1)}, f32[8,64,256]{2,1,0:T(8,128)S(1)}, u32[]{:S(2)}, u32[]{:S(2)}) %collective-permute-start.1) | collective-permute-done | bytes 524320 | tf_op jit(solution)/shard_map/ppermute | solution.py:302
  36.3 6.4 %collective-permute-done.2.rest_2_ = f32[64,8,256]{2,1,0:T(8,128)S(1)} collective-permute-done((f32[64,8,256]{2,1,0:T(8,128)}, f32[64,8,256]{2,1,0:T(8,128)S(1)}, u32[]{:S(2)}, u32[]{:S(2)}) %collective-permute-start.2) | collective-permute-done | bytes 524320 | tf_op jit(solution)/shard_map/ppermute | solution.py:302
  42.6 4.1 %collective-permute-done.3.rest_3_ = f32[64,8,256]{2,1,0:T(8,128)S(1)} collective-permute-done((f32[64,8,256]{2,1,0:T(8,128)S(1)}, f32[64,8,256]{2,1,0:T(8,128)S(1)}, u32[]{:S(2)}, u32[]{:S(2)}) %collective-permute-start.3) | collective-permute-done | bytes 524320 | tf_op jit(solution)/shard_map/ppermute | solution.py:302
  46.8 0.8 copy-done.8
  47.5 16.3 %dual.1 = (f32[64,64,256]{2,1,0:T(8,128)}, f32[64,64,256]{2,1,0:T(8,128)}, f32[8,64,256]{2,1,0:T(8,128)S(1)}, f32[8,64,256]{2,1,0:T(8,128)S(1)}, f32[64,8,256]{2...) custom-call(s32[3]{0:T(128)S(1)} %copy-done, ...), custom_call_target="tpu_custom_call" | custom-call | flops 3623878656 | bytes 21495808 | tf_op jit(solution)/shard_map/dual/pallas_call | solution.py:283
  63.9 4.3 %collective-permute-start.12 = (f32[8,8,256]{2,1,0:T(8,128)S(1)}, f32[8,8,256]{2,1,0:T(8,128)S(1)}, u32[]{:S(2)}, u32[]{:S(2)}) collective-permute-start(f32[8,8,256]{2,1,0:T(8,128)S(1)} %get-tuple-element.46), channel_id=1, source_target_pairs={{0,5},{1,6},{2,7},{4,9},{5,10},{6,11},{8,13},{9,14},{10,15},{16,21... | collective-permute-start | bytes 196616 | tf_op jit(solution)/shard_map/ppermute | solution.py:302
  68.2 1.3 collective-permute-start.13
  69.5 4.3 %collective-permute-start.14 = (f32[8,8,256]{2,1,0:T(8,128)S(1)}, f32[8,8,256]{2,1,0:T(8,128)S(1)}, u32[]{:S(2)}, u32[]{:S(2)}) collective-permute-start(f32[8,8,256]{2,1,0:T(8,128)S(1)} %get-tuple-element.48), channel_id=1, source_target_pairs={{4,1},{5,2},{6,3},{8,5},{9,6},{10,7},{12,9},{13,10},{14,11},{20,17... | collective-permute-start | bytes 196616 | tf_op jit(solution)/shard_map/ppermute | solution.py:302
  73.8 1.3 collective-permute-start.15
  75.1 2.9 %collective-permute-start.8 = (f32[8,64,256]{2,1,0:T(8,128)S(1)}, f32[8,64,256]{2,1,0:T(8,128)}, u32[]{:S(2)}, u32[]{:S(2)}) collective-permute-start(f32[8,64,256]{2,1,0:T(8,128)S(1)} %get-tuple-element.42), channel_id=1, source_target_pairs={{0,4},{1,5},{2,6},{3,7},{4,8},{5,9},{6,10},{7,11},{8,12},{9,13},{1... | collective-permute-start | bytes 1572872 | tf_op jit(solution)/shard_map/ppermute | solution.py:302
  78.0 2.2 %collective-permute-start.9 = (f32[8,64,256]{2,1,0:T(8,128)S(1)}, f32[8,64,256]{2,1,0:T(8,128)}, u32[]{:S(2)}, u32[]{:S(2)}) collective-permute-start(f32[8,64,256]{2,1,0:T(8,128)S(1)} %get-tuple-element.43), channel_id=1, source_target_pairs={{4,0},{5,1},{6,2},{7,3},{8,4},{9,5},{10,6},{11,7},{12,8},{13,9},{1... | collective-permute-start | bytes 1572872 | tf_op jit(solution)/shard_map/ppermute | solution.py:302
  80.2 5.0 %collective-permute-start.10 = (f32[64,8,256]{2,1,0:T(8,128)}, f32[64,8,256]{2,1,0:T(8,128)}, u32[]{:S(2)}, u32[]{:S(2)}) collective-permute-start(f32[64,8,256]{2,1,0:T(8,128)} %get-tuple-element.44), channel_id=1, source_target_pairs={{0,1},{1,2},{2,3},{4,5},{5,6},{6,7},{8,9},{9,10},{10,11},{12,13},{... | collective-permute-start | bytes 1572872 | tf_op jit(solution)/shard_map/ppermute | solution.py:302
  85.2 1.3 collective-permute-start.11
  87.1 1.5 collective-permute-done.9.rest_1_
  88.6 7.3 %collective-permute-done.10.rest_2_ = f32[64,8,256]{2,1,0:T(8,128)} collective-permute-done((f32[64,8,256]{2,1,0:T(8,128)}, f32[64,8,256]{2,1,0:T(8,128)}, u32[]{:S(2)}, u32[]{:S(2)}) %collective-permute-start.10) | collective-permute-done | bytes 524320 | tf_op jit(solution)/shard_map/ppermute | solution.py:302
  95.9 4.9 %collective-permute-done.11.rest_3_ = f32[64,8,256]{2,1,0:T(8,128)} collective-permute-done((f32[64,8,256]{2,1,0:T(8,128)}, f32[64,8,256]{2,1,0:T(8,128)}, u32[]{:S(2)}, u32[]{:S(2)}) %collective-permute-start.11) | collective-permute-done | bytes 524320 | tf_op jit(solution)/shard_map/ppermute | solution.py:302
  100.9 1.3 copy-done.2
  102.2 17.0 %partial.1 = (f32[64,64,128]{2,1,0:T(8,128)}, f32[64,64,128]{2,1,0:T(8,128)}, f32[64,64,256]{2,1,0:T(8,128)}, f32[8,64,256]{2,1,0:T(8,128)S(1)}, f32[8,64,256]{2...) custom-call(s32[3]{0:T(128)S(1)} %copy-done.1, ...), custom_call_target="tpu_custom_call" | custom-call | flops 3623878656 | bytes 25690112 | tf_op jit(solution)/shard_map/partial/pallas_call | solution.py:283
  119.2 0.2 collective-permute-start.17
  119.4 4.1 %collective-permute-start.22 = (f32[8,8,256]{2,1,0:T(8,128)S(1)}, f32[8,8,256]{2,1,0:T(8,128)S(1)}, u32[]{:S(2)}, u32[]{:S(2)}) collective-permute-start(f32[8,8,256]{2,1,0:T(8,128)S(1)} %get-tuple-element.57), channel_id=1, source_target_pairs={{0,5},{1,6},{2,7},{4,9},{5,10},{6,11},{8,13},{9,14},{10,15},{16,21... | collective-permute-start | bytes 196616 | tf_op jit(solution)/shard_map/ppermute | solution.py:302
  123.5 1.3 collective-permute-start.23
  124.8 4.3 %collective-permute-start.24 = (f32[8,8,256]{2,1,0:T(8,128)S(1)}, f32[8,8,256]{2,1,0:T(8,128)S(1)}, u32[]{:S(2)}, u32[]{:S(2)}) collective-permute-start(f32[8,8,256]{2,1,0:T(8,128)S(1)} %get-tuple-element.59), channel_id=1, source_target_pairs={{4,1},{5,2},{6,3},{8,5},{9,6},{10,7},{12,9},{13,10},{14,11},{20,17... | collective-permute-start | bytes 196616 | tf_op jit(solution)/shard_map/ppermute | solution.py:302
  129.1 1.3 collective-permute-start.25
  130.4 2.0 %collective-permute-start.18 = (f32[8,64,256]{2,1,0:T(8,128)S(1)}, f32[8,64,256]{2,1,0:T(8,128)S(1)}, u32[]{:S(2)}, u32[]{:S(2)}) collective-permute-start(f32[8,64,256]{2,1,0:T(8,128)S(1)} %get-tuple-element.53), channel_id=1, source_target_pairs={{0,4},{1,5},{2,6},{3,7},{4,8},{5,9},{6,10},{7,11},{8,12},{9,13},{1... | collective-permute-start | bytes 1572872 | tf_op jit(solution)/shard_map/ppermute | solution.py:302
  132.4 2.4 %collective-permute-start.19 = (f32[8,64,256]{2,1,0:T(8,128)S(1)}, f32[8,64,256]{2,1,0:T(8,128)S(1)}, u32[]{:S(2)}, u32[]{:S(2)}) collective-permute-start(f32[8,64,256]{2,1,0:T(8,128)S(1)} %get-tuple-element.54), channel_id=1, source_target_pairs={{4,0},{5,1},{6,2},{7,3},{8,4},{9,5},{10,6},{11,7},{12,8},{13,9},{1... | collective-permute-start | bytes 1572872 | tf_op jit(solution)/shard_map/ppermute | solution.py:302
  134.8 5.0 %collective-permute-start.20 = (f32[64,8,256]{2,1,0:T(8,128)}, f32[64,8,256]{2,1,0:T(8,128)S(1)}, u32[]{:S(2)}, u32[]{:S(2)}) collective-permute-start(f32[64,8,256]{2,1,0:T(8,128)} %get-tuple-element.55), channel_id=1, source_target_pairs={{0,1},{1,2},{2,3},{4,5},{5,6},{6,7},{8,9},{9,10},{10,11},{12,13},{... | collective-permute-start | bytes 1572872 | tf_op jit(solution)/shard_map/ppermute | solution.py:302
  139.7 1.3 collective-permute-start.21
  141.1 2.1 %collective-permute-done.19.rest_1_ = f32[8,64,256]{2,1,0:T(8,128)S(1)} collective-permute-done((f32[8,64,256]{2,1,0:T(8,128)S(1)}, f32[8,64,256]{2,1,0:T(8,128)S(1)}, u32[]{:S(2)}, u32[]{:S(2)}) %collective-permute-start.19) | collective-permute-done | bytes 524320 | tf_op jit(solution)/shard_map/ppermute | solution.py:302
  143.2 6.2 %collective-permute-done.20.rest_2_ = f32[64,8,256]{2,1,0:T(8,128)S(1)} collective-permute-done((f32[64,8,256]{2,1,0:T(8,128)}, f32[64,8,256]{2,1,0:T(8,128)S(1)}, u32[]{:S(2)}, u32[]{:S(2)}) %collective-permute-start.20) | collective-permute-done | bytes 524320 | tf_op jit(solution)/shard_map/ppermute | solution.py:302
  149.4 4.3 %collective-permute-done.21.rest_3_ = f32[64,8,256]{2,1,0:T(8,128)S(1)} collective-permute-done((f32[64,8,256]{2,1,0:T(8,128)}, f32[64,8,256]{2,1,0:T(8,128)S(1)}, u32[]{:S(2)}, u32[]{:S(2)}) %collective-permute-start.21) | collective-permute-done | bytes 524320 | tf_op jit(solution)/shard_map/ppermute | solution.py:302
  153.7 0.8 copy-done.4
  154.5 12.2 %gradient.1 = f32[64,64,256]{2,1,0:T(8,128)} custom-call(s32[3]{0:T(128)S(1)} %copy-done.1, f32[64,64,256]{2,1,0:T(8,128)} %get-tuple-element.52.u, f32[8,64,256]{2,1,0:T(8,128)S(1)} %collective-permute-done.18.rest_0_, f32[8,64,256]{2,1,0:T(8,128)S(1)} %collective-permute-done.19.rest_1_, f32[64,8,256]{2,1,0:T(8,128)S(1)} %collective-permute-done.20.rest_2_, ...), custom_call_target="tpu_custom_call" | custom-call | flops 2013265920 | bytes 14942208 | tf_op jit(solution)/shard_map/gradient/pallas_call | solution.py:283
  166.7 1.3 copy-done.3
  168.1 6.0 %barycenter.1 = f32[64,64,128]{2,1,0:T(8,128)} custom-call(f32[64,64,128]{2,1,0:T(8,128)} %get-tuple-element.50.a, f32[64,64,128]{2,1,0:T(8,128)} %copy-done.3), custom_call_target="tpu_custom_call" | custom-call | flops 524288 | bytes 6291456 | tf_op jit(solution)/shard_map/barycenter/pallas_call | solution.py:368
  (27 shorter events, 0.1 us)
Async XLA Ops:
  0.6 100.2 %collective-permute-start.16 = (f32[64,64,128]{2,1,0:T(8,128)}, f32[64,64,128]{2,1,0:T(8,128)S(1)}, u32[]{:S(2)}, u32[]{:S(2)}) collective-permute-start(f32[64,64,128]{2,1,0:T(8,128)} %rest_9_.1), channel_id=1, source_target_pairs={{0,16},{16,0},{1,17},{17,1},{2,18},{18,2},{3,19},{19,3},{4,20},{20... | collective-permute-start | bytes 6291464 | tf_op jit(solution)/shard_map/ppermute | solution.py:343
  2.8 0.7 copy-start
  10.6 11.9 %collective-permute-start.4 = (f32[8,8,256]{2,1,0:T(8,128)S(1)}, f32[8,8,256]{2,1,0:T(8,128)S(1)}, u32[]{:S(2)}, u32[]{:S(2)}) collective-permute-start(f32[8,8,256]{2,1,0:T(8,128)S(1)} %get-tuple-element.37), channel_id=1, source_target_pairs={{0,5},{1,6},{2,7},{4,9},{5,10},{6,11},{8,13},{9,14},{10,15},{16,21... | collective-permute-start | bytes 196616 | tf_op jit(solution)/shard_map/ppermute | solution.py:302
  15.6 9.8 %collective-permute-start.5 = (f32[8,8,256]{2,1,0:T(8,128)S(1)}, f32[8,8,256]{2,1,0:T(8,128)S(1)}, u32[]{:S(2)}, u32[]{:S(2)}) collective-permute-start(f32[8,8,256]{2,1,0:T(8,128)S(1)} %get-tuple-element.38), channel_id=1, source_target_pairs={{1,4},{2,5},{3,6},{5,8},{6,9},{7,10},{9,12},{10,13},{11,14},{17,20... | collective-permute-start | bytes 196616 | tf_op jit(solution)/shard_map/ppermute | solution.py:302
  16.9 10.5 %collective-permute-start.6 = (f32[8,8,256]{2,1,0:T(8,128)S(1)}, f32[8,8,256]{2,1,0:T(8,128)S(1)}, u32[]{:S(2)}, u32[]{:S(2)}) collective-permute-start(f32[8,8,256]{2,1,0:T(8,128)S(1)} %get-tuple-element.39), channel_id=1, source_target_pairs={{4,1},{5,2},{6,3},{8,5},{9,6},{10,7},{12,9},{13,10},{14,11},{20,17... | collective-permute-start | bytes 196616 | tf_op jit(solution)/shard_map/ppermute | solution.py:302
  21.2 10.7 %collective-permute-start.7 = (f32[8,8,256]{2,1,0:T(8,128)S(1)}, f32[8,8,256]{2,1,0:T(8,128)S(1)}, u32[]{:S(2)}, u32[]{:S(2)}) collective-permute-start(f32[8,8,256]{2,1,0:T(8,128)S(1)} %get-tuple-element.40), channel_id=1, source_target_pairs={{5,0},{6,1},{7,2},{9,4},{10,5},{11,6},{13,8},{14,9},{15,10},{21,16... | collective-permute-start | bytes 196616 | tf_op jit(solution)/shard_map/ppermute | solution.py:302
  22.5 10.7 %collective-permute-start = (f32[8,64,256]{2,1,0:T(8,128)S(1)}, f32[8,64,256]{2,1,0:T(8,128)S(1)}, u32[]{:S(2)}, u32[]{:S(2)}) collective-permute-start(f32[8,64,256]{2,1,0:T(8,128)S(1)} %get-tuple-element.33), channel_id=1, source_target_pairs={{0,4},{1,5},{2,6},{3,7},{4,8},{5,9},{6,10},{7,11},{8,12},{9,13},{1... | collective-permute-start | bytes 1572872 | tf_op jit(solution)/shard_map/ppermute | solution.py:302
  25.5 10.8 %collective-permute-start.1 = (f32[8,64,256]{2,1,0:T(8,128)S(1)}, f32[8,64,256]{2,1,0:T(8,128)S(1)}, u32[]{:S(2)}, u32[]{:S(2)}) collective-permute-start(f32[8,64,256]{2,1,0:T(8,128)S(1)} %get-tuple-element.34), channel_id=1, source_target_pairs={{4,0},{5,1},{6,2},{7,3},{8,4},{9,5},{10,6},{11,7},{12,8},{13,9},{1... | collective-permute-start | bytes 1572872 | tf_op jit(solution)/shard_map/ppermute | solution.py:302
  27.4 15.2 %collective-permute-start.2 = (f32[64,8,256]{2,1,0:T(8,128)}, f32[64,8,256]{2,1,0:T(8,128)S(1)}, u32[]{:S(2)}, u32[]{:S(2)}) collective-permute-start(f32[64,8,256]{2,1,0:T(8,128)} %get-tuple-element.35), channel_id=1, source_target_pairs={{0,1},{1,2},{2,3},{4,5},{5,6},{6,7},{8,9},{9,10},{10,11},{12,13},{... | collective-permute-start | bytes 1572872 | tf_op jit(solution)/shard_map/ppermute | solution.py:302
  31.9 14.9 %collective-permute-start.3 = (f32[64,8,256]{2,1,0:T(8,128)S(1)}, f32[64,8,256]{2,1,0:T(8,128)S(1)}, u32[]{:S(2)}, u32[]{:S(2)}) collective-permute-start(f32[64,8,256]{2,1,0:T(8,128)S(1)} %get-tuple-element.36), channel_id=1, source_target_pairs={{1,0},{2,1},{3,2},{5,4},{6,5},{7,6},{9,8},{10,9},{11,10},{13,12},{... | collective-permute-start | bytes 1572872 | tf_op jit(solution)/shard_map/ppermute | solution.py:302
  33.2 13.6 %copy-start.5 = (f32[8,64,256]{2,1,0:T(8,128)}, f32[8,64,256]{2,1,0:T(8,128)S(1)}, u32[]{:S(2)}) copy-start(f32[8,64,256]{2,1,0:T(8,128)S(1)} %collective-permute-done.rest_0_) | copy-start | bytes 1572868
  36.3 10.5 %copy-start.6 = (f32[8,64,256]{2,1,0:T(8,128)}, f32[8,64,256]{2,1,0:T(8,128)S(1)}, u32[]{:S(2)}) copy-start(f32[8,64,256]{2,1,0:T(8,128)S(1)} %collective-permute-done.1.rest_1_) | copy-start | bytes 1572868
  42.6 4.1 %copy-start.7 = (f32[64,8,256]{2,1,0:T(8,128)}, f32[64,8,256]{2,1,0:T(8,128)S(1)}, u32[]{:S(2)}) copy-start(f32[64,8,256]{2,1,0:T(8,128)S(1)} %collective-permute-done.2.rest_2_) | copy-start | bytes 1572868
  46.7 0.8 copy-start.8
  47.5 54.7 %copy-start.1 = (s32[3]{0:T(128)S(1)}, s32[3]{0:T(128)}, u32[]{:S(2)}) copy-start(s32[3]{0:T(128)} %reach.7) | copy-start | bytes 40
  63.9 11.2 %collective-permute-start.12 = (f32[8,8,256]{2,1,0:T(8,128)S(1)}, f32[8,8,256]{2,1,0:T(8,128)S(1)}, u32[]{:S(2)}, u32[]{:S(2)}) collective-permute-start(f32[8,8,256]{2,1,0:T(8,128)S(1)} %get-tuple-element.46), channel_id=1, source_target_pairs={{0,5},{1,6},{2,7},{4,9},{5,10},{6,11},{8,13},{9,14},{10,15},{16,21... | collective-permute-start | bytes 196616 | tf_op jit(solution)/shard_map/ppermute | solution.py:302
  68.2 9.8 %collective-permute-start.13 = (f32[8,8,256]{2,1,0:T(8,128)S(1)}, f32[8,8,256]{2,1,0:T(8,128)S(1)}, u32[]{:S(2)}, u32[]{:S(2)}) collective-permute-start(f32[8,8,256]{2,1,0:T(8,128)S(1)} %get-tuple-element.47), channel_id=1, source_target_pairs={{1,4},{2,5},{3,6},{5,8},{6,9},{7,10},{9,12},{10,13},{11,14},{17,20... | collective-permute-start | bytes 196616 | tf_op jit(solution)/shard_map/ppermute | solution.py:302
  69.5 10.7 %collective-permute-start.14 = (f32[8,8,256]{2,1,0:T(8,128)S(1)}, f32[8,8,256]{2,1,0:T(8,128)S(1)}, u32[]{:S(2)}, u32[]{:S(2)}) collective-permute-start(f32[8,8,256]{2,1,0:T(8,128)S(1)} %get-tuple-element.48), channel_id=1, source_target_pairs={{4,1},{5,2},{6,3},{8,5},{9,6},{10,7},{12,9},{13,10},{14,11},{20,17... | collective-permute-start | bytes 196616 | tf_op jit(solution)/shard_map/ppermute | solution.py:302
  73.8 11.4 %collective-permute-start.15 = (f32[8,8,256]{2,1,0:T(8,128)S(1)}, f32[8,8,256]{2,1,0:T(8,128)S(1)}, u32[]{:S(2)}, u32[]{:S(2)}) collective-permute-start(f32[8,8,256]{2,1,0:T(8,128)S(1)} %get-tuple-element.49), channel_id=1, source_target_pairs={{5,0},{6,1},{7,2},{9,4},{10,5},{11,6},{13,8},{14,9},{15,10},{21,16... | collective-permute-start | bytes 196616 | tf_op jit(solution)/shard_map/ppermute | solution.py:302
  75.1 12.1 %collective-permute-start.8 = (f32[8,64,256]{2,1,0:T(8,128)S(1)}, f32[8,64,256]{2,1,0:T(8,128)}, u32[]{:S(2)}, u32[]{:S(2)}) collective-permute-start(f32[8,64,256]{2,1,0:T(8,128)S(1)} %get-tuple-element.42), channel_id=1, source_target_pairs={{0,4},{1,5},{2,6},{3,7},{4,8},{5,9},{6,10},{7,11},{8,12},{9,13},{1... | collective-permute-start | bytes 1572872 | tf_op jit(solution)/shard_map/ppermute | solution.py:302
  78.0 10.6 %collective-permute-start.9 = (f32[8,64,256]{2,1,0:T(8,128)S(1)}, f32[8,64,256]{2,1,0:T(8,128)}, u32[]{:S(2)}, u32[]{:S(2)}) collective-permute-start(f32[8,64,256]{2,1,0:T(8,128)S(1)} %get-tuple-element.43), channel_id=1, source_target_pairs={{4,0},{5,1},{6,2},{7,3},{8,4},{9,5},{10,6},{11,7},{12,8},{13,9},{1... | collective-permute-start | bytes 1572872 | tf_op jit(solution)/shard_map/ppermute | solution.py:302
  80.2 15.7 %collective-permute-start.10 = (f32[64,8,256]{2,1,0:T(8,128)}, f32[64,8,256]{2,1,0:T(8,128)}, u32[]{:S(2)}, u32[]{:S(2)}) collective-permute-start(f32[64,8,256]{2,1,0:T(8,128)} %get-tuple-element.44), channel_id=1, source_target_pairs={{0,1},{1,2},{2,3},{4,5},{5,6},{6,7},{8,9},{9,10},{10,11},{12,13},{... | collective-permute-start | bytes 1572872 | tf_op jit(solution)/shard_map/ppermute | solution.py:302
  85.2 15.7 %collective-permute-start.11 = (f32[64,8,256]{2,1,0:T(8,128)}, f32[64,8,256]{2,1,0:T(8,128)}, u32[]{:S(2)}, u32[]{:S(2)}) collective-permute-start(f32[64,8,256]{2,1,0:T(8,128)} %get-tuple-element.45), channel_id=1, source_target_pairs={{1,0},{2,1},{3,2},{5,4},{6,5},{7,6},{9,8},{10,9},{11,10},{13,12},{... | collective-permute-start | bytes 1572872 | tf_op jit(solution)/shard_map/ppermute | solution.py:302
  100.9 1.3 copy-start.2
  119.2 47.5 %collective-permute-start.17 = (f32[64,64,128]{2,1,0:T(8,128)}, f32[64,64,128]{2,1,0:T(8,128)S(1)}, u32[]{:S(2)}, u32[]{:S(2)}) collective-permute-start(f32[64,64,128]{2,1,0:T(8,128)} %get-tuple-element.51), channel_id=1, source_target_pairs={{0,16},{16,0},{1,17},{17,1},{2,18},{18,2},{3,19},{19,3},{4,20},{20... | collective-permute-start | bytes 6291464 | tf_op jit(solution)/shard_map/ppermute | solution.py:360
  119.4 10.9 %collective-permute-start.22 = (f32[8,8,256]{2,1,0:T(8,128)S(1)}, f32[8,8,256]{2,1,0:T(8,128)S(1)}, u32[]{:S(2)}, u32[]{:S(2)}) collective-permute-start(f32[8,8,256]{2,1,0:T(8,128)S(1)} %get-tuple-element.57), channel_id=1, source_target_pairs={{0,5},{1,6},{2,7},{4,9},{5,10},{6,11},{8,13},{9,14},{10,15},{16,21... | collective-permute-start | bytes 196616 | tf_op jit(solution)/shard_map/ppermute | solution.py:302
  123.5 8.9 %collective-permute-start.23 = (f32[8,8,256]{2,1,0:T(8,128)S(1)}, f32[8,8,256]{2,1,0:T(8,128)S(1)}, u32[]{:S(2)}, u32[]{:S(2)}) collective-permute-start(f32[8,8,256]{2,1,0:T(8,128)S(1)} %get-tuple-element.58), channel_id=1, source_target_pairs={{1,4},{2,5},{3,6},{5,8},{6,9},{7,10},{9,12},{10,13},{11,14},{17,20... | collective-permute-start | bytes 196616 | tf_op jit(solution)/shard_map/ppermute | solution.py:302
  124.8 10.0 %collective-permute-start.24 = (f32[8,8,256]{2,1,0:T(8,128)S(1)}, f32[8,8,256]{2,1,0:T(8,128)S(1)}, u32[]{:S(2)}, u32[]{:S(2)}) collective-permute-start(f32[8,8,256]{2,1,0:T(8,128)S(1)} %get-tuple-element.59), channel_id=1, source_target_pairs={{4,1},{5,2},{6,3},{8,5},{9,6},{10,7},{12,9},{13,10},{14,11},{20,17... | collective-permute-start | bytes 196616 | tf_op jit(solution)/shard_map/ppermute | solution.py:302
  129.1 10.7 %collective-permute-start.25 = (f32[8,8,256]{2,1,0:T(8,128)S(1)}, f32[8,8,256]{2,1,0:T(8,128)S(1)}, u32[]{:S(2)}, u32[]{:S(2)}) collective-permute-start(f32[8,8,256]{2,1,0:T(8,128)S(1)} %get-tuple-element.60), channel_id=1, source_target_pairs={{5,0},{6,1},{7,2},{9,4},{10,5},{11,6},{13,8},{14,9},{15,10},{21,16... | collective-permute-start | bytes 196616 | tf_op jit(solution)/shard_map/ppermute | solution.py:302
  130.4 10.7 %collective-permute-start.18 = (f32[8,64,256]{2,1,0:T(8,128)S(1)}, f32[8,64,256]{2,1,0:T(8,128)S(1)}, u32[]{:S(2)}, u32[]{:S(2)}) collective-permute-start(f32[8,64,256]{2,1,0:T(8,128)S(1)} %get-tuple-element.53), channel_id=1, source_target_pairs={{0,4},{1,5},{2,6},{3,7},{4,8},{5,9},{6,10},{7,11},{8,12},{9,13},{1... | collective-permute-start | bytes 1572872 | tf_op jit(solution)/shard_map/ppermute | solution.py:302
  132.4 10.8 %collective-permute-start.19 = (f32[8,64,256]{2,1,0:T(8,128)S(1)}, f32[8,64,256]{2,1,0:T(8,128)S(1)}, u32[]{:S(2)}, u32[]{:S(2)}) collective-permute-start(f32[8,64,256]{2,1,0:T(8,128)S(1)} %get-tuple-element.54), channel_id=1, source_target_pairs={{4,0},{5,1},{6,2},{7,3},{8,4},{9,5},{10,6},{11,7},{12,8},{13,9},{1... | collective-permute-start | bytes 1572872 | tf_op jit(solution)/shard_map/ppermute | solution.py:302
  134.8 14.6 %collective-permute-start.20 = (f32[64,8,256]{2,1,0:T(8,128)}, f32[64,8,256]{2,1,0:T(8,128)S(1)}, u32[]{:S(2)}, u32[]{:S(2)}) collective-permute-start(f32[64,8,256]{2,1,0:T(8,128)} %get-tuple-element.55), channel_id=1, source_target_pairs={{0,1},{1,2},{2,3},{4,5},{5,6},{6,7},{8,9},{9,10},{10,11},{12,13},{... | collective-permute-start | bytes 1572872 | tf_op jit(solution)/shard_map/ppermute | solution.py:302
  139.7 14.0 %collective-permute-start.21 = (f32[64,8,256]{2,1,0:T(8,128)}, f32[64,8,256]{2,1,0:T(8,128)S(1)}, u32[]{:S(2)}, u32[]{:S(2)}) collective-permute-start(f32[64,8,256]{2,1,0:T(8,128)} %get-tuple-element.56), channel_id=1, source_target_pairs={{1,0},{2,1},{3,2},{5,4},{6,5},{7,6},{9,8},{10,9},{11,10},{13,12},{... | collective-permute-start | bytes 1572872 | tf_op jit(solution)/shard_map/ppermute | solution.py:302
  153.7 0.8 copy-start.4
  166.7 1.4 copy-start.3
